TPU v7x, 256 devices: a whole 4x4x8 slice. The times are simulated.
256 devices in a mesh: seq: 32 (over x, y, core), vid: 8 (over z).
Axes of the slice: x: 4, y: 4, z: 8, core: 2. Of those that a mesh axis runs over, the one named last changes fastest.
Arguments:
- tokens: bfloat16 [262144, 768], P(('vid', 'seq')), parts along dimension 0, may hold values from -100 to 100
- latents: bfloat16 [4096, 768], P(('vid', 'seq')), parts along dimension 0, may hold values from -6 to 6
- read_weights: bfloat16 [4, 768, 768], P(None, 'seq'), may hold values from -1 to 1
- later_weights: bfloat16 [8, 768, 768], P(None, 'seq'), may hold values from -1 to 1
- head_scale: float32 [3, 12], replicated, may hold values from 1 to 40
Outputs:
- tokens_out: bfloat16 [262144, 768], P(('vid', 'seq')), parts along dimension 0
- latents_out: float32 [4096, 768], P(('vid', 'seq')), parts along dimension 0
There are 8 independent parts, one for each index of `vid`. A program takes and returns all parts, laid end to end along the dimension named above; an argument that names none is the same for every part. Nothing has to cross between parts.
All inputs are finite; a program needn't handle non-finite values.
Results may differ from a plain program's by a relative error of at most 0.01.
The roundings to bfloat16 on the way count: a program that leaves them out, or rounds other values in their place, can miss the bound.
Values may be sent and summed in bfloat16 or wider, within the bound.
No kernel may reach another device: no remote copies, remote signals or barrier semaphores. Data moves between devices by JAX's collectives and lax.ppermute only.
A program may use at most 64 MiB of HBM per device.

v0:
```python
import functools
import math

import jax
import jax.numpy as jnp
from jax import lax
from jax.experimental import pallas as pl
from jax.experimental.pallas import tpu as pltpu
from jax.sharding import PartitionSpec as P

HEADS = 12
HEAD_DIM = 64
PAIR = 2 * HEAD_DIM
EPSILON = 1e-06
LOG2E = math.log2(math.e)
BF16 = jnp.bfloat16
F32 = jnp.float32
MIB = 1024 * 1024
PACK_VMEM = 58 * MIB
READ_VMEM = 56 * MIB
COMBINE_VMEM = 40 * MIB
QUERY_VMEM = 50 * MIB
WRITE_VMEM = 50 * MIB
PIECE = 16
TOTALS = 6
CORES = 2
WRITE_UNROLL = 4


def norm_rows(values):
    values = values.astype(F32)
    return values * lax.rsqrt(jnp.mean(values * values, axis=-1, keepdims=True) + EPSILON)


def dot(left, right):
    return jnp.dot(left, right, preferred_element_type=F32)


def dot_nt(left, right):
    return lax.dot_general(left, right, (((1,), (1,)), ((), ())), preferred_element_type=F32)


def head_mean_matrix():
    rows = lax.broadcasted_iota(jnp.int32, (256, 256), 0) // HEAD_DIM
    cols = lax.broadcasted_iota(jnp.int32, (256, 256), 1) // HEAD_DIM
    return jnp.where(rows == cols, 1.0 / HEAD_DIM, 0.0).astype(BF16)


def head_norm(values, mean_matrix):
    squares = values * values
    high = squares.astype(BF16)
    low = (squares - high.astype(F32)).astype(BF16)
    parts = []
    for start in range(0, values.shape[1], 256):
        cols = slice(start, min(start + 256, values.shape[1]))
        size = cols.stop - start
        matrix = mean_matrix[:size, :size]
        mean = dot(high[:, cols], matrix) + dot(low[:, cols], matrix)
        parts.append((values[:, cols] * lax.rsqrt(mean + EPSILON)).astype(BF16))
    return jnp.concatenate(parts, axis=1)


def first_half(shape):
    return lax.broadcasted_iota(jnp.int32, shape, 1) % PAIR < HEAD_DIM


def row_blocks(n_rows, block, body):
    for start in range(0, n_rows, block):
        body(pl.ds(start, block))


def project_heads(x_ref, weight, mean_matrix, out_ref, block=512):
    def body(rows):
        out_ref[rows, :] = head_norm(dot(x_ref[rows, :], weight[...]), mean_matrix)

    row_blocks(x_ref.shape[0], block, body)


def project_values(x_ref, weight, out_ref, block=512):
    def body(rows):
        out_ref[rows, :] = dot(x_ref[rows, :], weight[...]).astype(BF16)

    row_blocks(x_ref.shape[0], block, body)


def attend(q_ref, k_ref, v_ref, factor, emit, block=512, unroll=1):
    n_blocks = q_ref.shape[0] // block
    n_steps = n_blocks * (q_ref.shape[1] // PAIR)

    def step(i, carry):
        pair, row = i // n_blocks, i % n_blocks
        cols, rows = pair * PAIR, row * block
        if not isinstance(i, int):
            cols, rows = pl.multiple_of(cols, PAIR), pl.multiple_of(rows, block)
        cols, rows = pl.ds(cols, PAIR), pl.ds(rows, block)
        queries, keys, values = q_ref[rows, cols], k_ref[:, cols], v_ref[:, cols]
        values = jnp.concatenate([values, jnp.ones_like(values)], axis=1)
        mask = first_half(queries.shape)
        zero = jnp.zeros_like(queries)
        heads = []
        for which in range(2):
            own = (mask, queries, zero) if which == 0 else (mask, zero, queries)
            scores = dot_nt(jnp.where(*own), keys)
            top = jnp.max(scores, axis=1, keepdims=True)
            weights = jnp.exp2((scores - top) * (factor(2 * pair + which) * LOG2E))
            both = dot(weights.astype(BF16), values)
            heads.append((top, both[:, :PAIR], both[:, PAIR:]))
        emit(pair, rows, cols, heads)
        return carry

    if unroll >= n_steps:
        for i in range(n_steps):
            step(i, 0)
    else:
        lax.fori_loop(0, n_steps, step, 0, unroll=unroll)


def attend_into(q_ref, k_ref, v_ref, scale_ref, stage, out_ref, unroll):
    def emit(pair, rows, cols, heads):
        (_, even, even_total), (_, odd, odd_total) = heads
        mask = first_half(even.shape)
        total = jnp.where(mask, even_total, odd_total)
        inverse = pl.reciprocal(total, approx=True)
        inverse = inverse * (2.0 - total * inverse)
        out_ref[rows, cols] = (jnp.where(mask, even, odd) * inverse).astype(BF16)

    def factor(head):
        return scale_ref[stage, head] / math.sqrt(HEAD_DIM)

    attend(q_ref, k_ref, v_ref, factor, emit, unroll=unroll)


def pack_kernel(read_ref, later_ref, lat_ref, first_ref, rest_ref):
    _, n_rows, width = read_ref.shape
    own_rows = lat_ref.shape[0]
    half = width // CORES
    rest_ref[0] = read_ref[3]
    rest_ref[1:] = later_ref[...]
    lat = lat_ref[...].astype(F32)
    split = own_rows * width // n_rows
    low = own_rows // 2
    extra = jnp.concatenate([lat[:low, split:], lat[low:, split:]], axis=1)
    extra = jnp.concatenate([lat[:, :split], extra], axis=0).astype(BF16)
    for core in range(CORES):
        cols = slice(core * half, (core + 1) * half)
        block = jnp.concatenate([read_ref[i][:, cols] for i in range(3)] + [extra], axis=1)
        first_ref[:, core] = jnp.broadcast_to(block[None], (first_ref.shape[0],) + block.shape)


def unpack_latents(blocks, own_rows, width):
    devices, n_rows, split = blocks.shape
    blocks = blocks.astype(F32)
    low = blocks[:, own_rows:]
    low = jnp.concatenate([low[:, :, : split // 2], low[:, :, split // 2 :]], axis=1)
    high = blocks[:, :own_rows].reshape(devices * own_rows, split)
    return jnp.concatenate([high, low.reshape(devices * own_rows, width - split)], axis=1)


def read_kernel(
    core_ref,
    scale_ref,
    own_hbm_ref,
    peer_hbm_ref,
    first_hbm_ref,
    block_hbm_ref,
    out_ref,
    lat_ref,
    tok_ref,
    weight_ref,
    block_ref,
    normed_ref,
    q_ref,
    k_ref,
    v_ref,
    extra_ref,
    sems,
):
    width = q_ref.shape[1]
    columns = [pl.ds(i * width, width) for i in range(3)]
    block_copy = pltpu.make_async_copy(
        block_hbm_ref.at[:, :, pl.ds(3 * width, block_ref.shape[2])], block_ref, sems.at[0]
    )
    weight_copies = [
        pltpu.make_async_copy(
            first_hbm_ref.at[:, columns[i]], weight_ref.at[:, columns[i]], sems.at[1 + i]
        )
        for i in range(3)
    ]
    n_tok = own_hbm_ref.shape[0]
    own_copy = pltpu.make_async_copy(own_hbm_ref, tok_ref.at[pl.ds(0, n_tok), :], sems.at[4])
    peer_copy = pltpu.make_async_copy(
        peer_hbm_ref, tok_ref.at[pl.ds(n_tok, n_tok), :], sems.at[5]
    )
    for copy in (block_copy, weight_copies[0], own_copy, *weight_copies[1:], peer_copy):
        copy.start()
    mean_matrix = head_mean_matrix()
    n_heads = width // HEAD_DIM
    n_lat, full_width = lat_ref.shape
    block_copy.wait()
    lat = unpack_latents(block_ref[...], n_lat // block_ref.shape[0], full_width)
    lat_ref[...] = lat.astype(BF16)
    normed_ref[...] = norm_rows(lat).astype(BF16)
    weight_copies[0].wait()
    project_heads(normed_ref, weight_ref.at[:, columns[0]], mean_matrix, q_ref)
    own_copy.wait()
    for copy in (*weight_copies[1:], peer_copy):
        copy.wait()

    def project_block(i, carry):
        rows = pl.ds(pl.multiple_of(i * 512, 512), 512)
        keys = dot(tok_ref[rows, :], weight_ref[:, columns[1]])
        k_ref[rows, :] = head_norm(keys, mean_matrix)
        v_ref[rows, :] = dot(tok_ref[rows, :], weight_ref[:, columns[2]]).astype(BF16)
        return carry

    lax.fori_loop(0, tok_ref.shape[0] // 512, project_block, 0)
    extra_ref[...] = jnp.zeros_like(extra_ref)

    def factor(head):
        return scale_ref[0, core_ref[0] * n_heads + head] / math.sqrt(HEAD_DIM)

    def emit(pair, rows, cols, heads):
        (_, even, _), (_, odd, _) = heads
        out_ref[rows, cols] = jnp.where(first_half(even.shape), even, odd).astype(BF16)
        lane = lax.broadcasted_iota(jnp.int32, even.shape, 1)
        extra = extra_ref[rows, :]
        for which, (top, _, total) in enumerate(heads):
            head = 2 * pair + which
            extra = jnp.where(lane == head, top * factor(head), extra)
            extra = jnp.where(lane == TOTALS + head, total, extra)
        extra_ref[rows, :] = extra

    attend(q_ref, k_ref, v_ref, factor, emit, unroll=3)
    extra = extra_ref[...]
    high = extra.astype(BF16).astype(F32)
    mid = (extra - high).astype(BF16).astype(F32)
    low = extra - high - mid
    packed = high + pltpu.roll(mid, PIECE, 1) + pltpu.roll(low, 2 * PIECE, 1)
    out_ref[:, width:] = packed.astype(BF16)


def combine_kernel(part_ref, out_ref, *, parts):
    width = out_ref.shape[-1]
    rows = out_ref.shape[1]
    lane = lax.broadcasted_iota(jnp.int32, (PAIR, width), 0)
    head = lax.broadcasted_iota(jnp.int32, (PAIR, width), 1) // HEAD_DIM
    pick_top = jnp.zeros((PAIR, width), F32)
    pick_total = jnp.zeros((PAIR, width), F32)
    for piece in range(3):
        pick_top = jnp.where(lane == head + piece * PIECE, 1.0, pick_top)
        pick_total = jnp.where(lane == head + TOTALS + piece * PIECE, 1.0, pick_total)
    extra = part_ref[:, width:]
    shape = (parts, rows, width)
    tops = dot(extra, pick_top.astype(BF16)).reshape(shape)
    totals = dot(extra, pick_total.astype(BF16)).reshape(shape)
    rescale = jnp.exp(tops - jnp.max(tops, axis=0, keepdims=True))
    sums = part_ref[:, :width].astype(F32).reshape(shape)
    mixed = jnp.sum(rescale * sums, axis=0) / jnp.sum(rescale * totals, axis=0)
    out_ref[...] = jnp.broadcast_to(mixed.astype(BF16)[None], out_ref.shape)


def query_kernel(tok_ref, weight_ref, out_ref):
    project_heads(tok_ref, weight_ref.at[0], head_mean_matrix(), out_ref)


READ_OUT, SELF_Q, SELF_K, SELF_V, SELF_OUT, WRITE_Q, WRITE_K, WRITE_V, WRITE_OUT = range(9)


def write_kernel(
    index_ref,
    scale_ref,
    mix_ref,
    lat_ref,
    weights_ref,
    raw_hbm_ref,
    query_hbm_ref,
    tok_out_ref,
    lat_out_ref,
    weight_ref,
    raw_ref,
    write_q_ref,
    stream_ref,
    normed_ref,
    q_ref,
    k_ref,
    v_ref,
    att_ref,
    write_att_ref,
    sems,
):
    order = (READ_OUT, SELF_Q, SELF_K, SELF_V, SELF_OUT, WRITE_K, WRITE_V, WRITE_OUT)
    copies = {}
    for slot, matrix in enumerate(order):
        copies[matrix] = pltpu.make_async_copy(
            weights_ref.at[matrix], weight_ref.at[slot], sems.at[slot]
        )
    query_copy = pltpu.make_async_copy(query_hbm_ref, write_q_ref, sems.at[len(order)])
    raw_copy = pltpu.make_async_copy(raw_hbm_ref, raw_ref, sems.at[len(order) + 1])
    for matrix in order:
        copies[matrix].start()
    query_copy.start()
    raw_copy.start()

    def ready(matrix):
        copies[matrix].wait()
        return weight_ref.at[order.index(matrix)]

    mean_matrix = head_mean_matrix()
    n_lat = lat_ref.shape[0]
    own_rows = lat_out_ref.shape[0]
    chips, cores, chip_rows, half = mix_ref.shape
    weight = ready(READ_OUT)
    lat_one = lat_ref[...].astype(F32)
    for core in range(cores):
        mix = mix_ref[:, core].reshape(chips * chip_rows, half)
        lat_one += dot(mix, weight[core * half : (core + 1) * half, :])
    stream_ref[...] = lat_one
    normed_ref[...] = norm_rows(lat_one).astype(BF16)
    project_heads(normed_ref, ready(SELF_Q), mean_matrix, q_ref)
    project_heads(normed_ref, ready(SELF_K), mean_matrix, k_ref)
    project_values(normed_ref, ready(SELF_V), v_ref)
    attend_into(q_ref, k_ref, v_ref, scale_ref, 1, att_ref, 6)
    lat_two = stream_ref[...] + dot(att_ref[...], ready(SELF_OUT)[...])
    stream_ref[...] = lat_two
    normed_ref[...] = norm_rows(lat_two).astype(BF16)
    own = pl.ds(pl.multiple_of(index_ref[0] * own_rows, own_rows), own_rows)
    lat_out_ref[...] = stream_ref[own, :]
    project_heads(normed_ref, ready(WRITE_K), mean_matrix, k_ref)
    project_values(normed_ref, ready(WRITE_V), v_ref)
    query_copy.wait()
    attend_into(write_q_ref, k_ref, v_ref, scale_ref, 2, write_att_ref, WRITE_UNROLL)
    weight = ready(WRITE_OUT)
    raw_copy.wait()

    def last(rows):
        update = dot(write_att_ref[rows, :], weight[...])
        tok_out_ref[rows, :] = (raw_ref[rows, :].astype(F32) + update).astype(BF16)

    row_blocks(raw_ref.shape[0], 512, last)


IN_VMEM = pl.BlockSpec(memory_space=pltpu.VMEM)
IN_SMEM = pl.BlockSpec(memory_space=pltpu.SMEM)
IN_PLACE = pl.BlockSpec(memory_space=pl.ANY)


def read_call(core, head_scale, own, peer, blocks, n_lat):
    n_tok, width = own.shape
    half = width // CORES
    devices, n_rows, packed_width = blocks.shape
    return pl.pallas_call(
        read_kernel,
        name="read",
        out_shape=(
            jax.ShapeDtypeStruct((n_lat, half + PAIR), BF16),
            jax.ShapeDtypeStruct((n_lat, width), BF16),
        ),
        in_specs=[IN_SMEM, IN_SMEM] + [IN_PLACE] * 4,
        out_specs=(IN_VMEM, IN_VMEM),
        scratch_shapes=[
            pltpu.VMEM((2 * n_tok, width), BF16),
            pltpu.VMEM((width, 3 * half), BF16),
            pltpu.VMEM((devices, n_rows, packed_width - 3 * half), BF16),
            pltpu.VMEM((n_lat, width), BF16),
            pltpu.VMEM((n_lat, half), BF16),
            pltpu.VMEM((2 * n_tok, half), BF16),
            pltpu.VMEM((2 * n_tok, half), BF16),
            pltpu.VMEM((n_lat, PAIR), F32),
            pltpu.SemaphoreType.DMA((6,)),
        ],
        compiler_params=pltpu.CompilerParams(vmem_limit_bytes=READ_VMEM),
        cost_estimate=pl.CostEstimate(
            flops=20_000_000_000, bytes_accessed=8_000_000, transcendentals=6_300_000
        ),
    )(core, head_scale, own, peer, blocks.reshape(devices * n_rows, packed_width), blocks)


def write_call(index, head_scale, mixed, lat_full, rest, tokens, queries, own_rows):
    n_lat, width = lat_full.shape
    latents_bf16 = pltpu.VMEM((n_lat, width), BF16)
    tokens_bf16 = pltpu.VMEM(tokens.shape, BF16)
    return pl.pallas_call(
        write_kernel,
        name="write",
        out_shape=(
            jax.ShapeDtypeStruct(tokens.shape, BF16),
            jax.ShapeDtypeStruct((own_rows, width), F32),
        ),
        in_specs=[IN_SMEM, IN_SMEM, IN_VMEM, IN_VMEM, IN_PLACE, IN_PLACE, IN_PLACE],
        out_specs=(IN_VMEM, IN_VMEM),
        scratch_shapes=[
            pltpu.VMEM((8, width, width), BF16),
            tokens_bf16,
            tokens_bf16,
            pltpu.VMEM((n_lat, width), F32),
            latents_bf16,
            latents_bf16,
            latents_bf16,
            latents_bf16,
            latents_bf16,
            tokens_bf16,
            pltpu.SemaphoreType.DMA((10,)),
        ],
        compiler_params=pltpu.CompilerParams(vmem_limit_bytes=WRITE_VMEM),
    )(index, head_scale, mixed, lat_full, rest, tokens, queries)


def shards(tokens, latents, read_weights, later_weights, head_scale):
    n_tok, width = tokens.shape
    own_rows = latents.shape[0]
    devices = lax.axis_size("seq")
    chips = devices // CORES
    n_lat = own_rows * devices
    half = width // CORES
    weight_rows = read_weights.shape[1]
    index = lax.axis_index("seq").astype(jnp.int32)
    same_core = [[CORES * chip + core for chip in range(chips)] for core in range(CORES)]
    swap = [(device, device ^ 1) for device in range(devices)]

    packed_width = 3 * half + own_rows * width // weight_rows
    first, rest = pl.pallas_call(
        pack_kernel,
        name="pack",
        out_shape=(
            jax.ShapeDtypeStruct((chips, CORES, weight_rows, packed_width), BF16),
            jax.ShapeDtypeStruct((9, weight_rows, width), BF16),
        ),
        in_specs=[IN_VMEM] * 3,
        out_specs=(IN_VMEM, IN_VMEM),
        compiler_params=pltpu.CompilerParams(vmem_limit_bytes=PACK_VMEM),
    )(read_weights, later_weights, latents)
    first = first.reshape(devices, weight_rows, packed_width)
    first = lax.all_to_all(first, "seq", 0, 0, tiled=True)
    rest = lax.all_gather(rest, "seq", axis=1, tiled=True)
    tok_normed = norm_rows(tokens).astype(BF16)
    peer_normed = lax.ppermute(tok_normed, "seq", swap)
    parts, lat_full = read_call(
        (index % CORES).reshape(1), head_scale, tok_normed, peer_normed, first, n_lat
    )
    queries = pl.pallas_call(
        query_kernel,
        name="query",
        grid=(1,),
        out_shape=jax.ShapeDtypeStruct((n_tok, width), BF16),
        in_specs=[
            pl.BlockSpec((n_tok, width), lambda i: (0, 0)),
            pl.BlockSpec((1, width, width), lambda i: (WRITE_Q, 0, 0)),
        ],
        out_specs=pl.BlockSpec((n_tok, width), lambda i: (0, 0)),
        compiler_params=pltpu.CompilerParams(vmem_limit_bytes=QUERY_VMEM),
        cost_estimate=pl.CostEstimate(
            flops=4_000_000_000, bytes_accessed=5_000_000, transcendentals=800_000
        ),
    )(tok_normed, rest)
    parts = lax.all_to_all(
        parts.reshape(chips, CORES * own_rows, half + PAIR),
        "seq",
        0,
        0,
        tiled=True,
        axis_index_groups=same_core,
    )
    mixed = pl.pallas_call(
        functools.partial(combine_kernel, parts=chips),
        name="combine",
        out_shape=jax.ShapeDtypeStruct((devices, CORES * own_rows, half), BF16),
        in_specs=[IN_VMEM],
        out_specs=IN_VMEM,
        compiler_params=pltpu.CompilerParams(vmem_limit_bytes=COMBINE_VMEM),
    )(parts.reshape(n_lat, half + PAIR))
    mixed = lax.all_to_all(mixed, "seq", 0, 0, tiled=True)
    mixed = mixed.reshape(chips, CORES, CORES * own_rows, half)
    return write_call(
        index.reshape(1), head_scale, mixed, lat_full, rest, tokens, queries, own_rows
    )


def solution(mesh):
    placed = (
        P(("vid", "seq"), None),
        P(("vid", "seq"), None),
        P(None, "seq", None),
        P(None, "seq", None),
        P(),
    )
    return jax.shard_map(
        shards,
        mesh=mesh,
        in_specs=placed,
        out_specs=(P(("vid", "seq"), None), P(("vid", "seq"), None)),
        check_vma=False,
    )
```

profile of v0, /device:TPU:1, one launch (start us, length us, event | category | flops | bytes accessed | tf_op | source)
XLA Modules:
  0.0 148.5 jit_solution(14187827003662927166)
XLA Ops:
  7.2 0.0 all-gather.2.cloned.1.call-start
  7.2 2.6 %pack.1 = (bf16[16,2,24,1664]{3,2,1,0:T(8,128)(2,1)}, bf16[9,24,768]{2,1,0:T(8,128)(2,1)}) custom-call(bf16[4,24,768]{2,1,0:T(8,128)(2,1)} %read_ref.1, bf16[8,24,768]{2,1,0:T(8,128)(2,1)} %later_ref.1, bf16[16,768]{1,0:T(8,128)(2,1)} %lat_ref.1), custom_call_target="tpu_custom_call" | custom-call | tf_op jit(solution)/shard_map/pack/pallas_call | solution.py:421
  9.8 0.0 all-gather.2.cloned.1.call-update
  9.9 0.0 copy-start
  9.9 8.8 %all-to-all-start = ((bf16[32,24,1664]{2,1,0:T(8,128)(2,1)}), bf16[32,24,1664]{2,1,0:T(8,128)(2,1)}, u32[]{:S(2)}, u32[]{:S(2)}) async-start(bf16[32,24,1664]{2,1,0:T(8,128)(2,1)} %bitcast.9), calls=%async_computation | async-start | bytes 5111808 | tf_op jit(solution)/shard_map/all_to_all | solution.py:433
  18.7 0.0 copy-done
  18.7 0.4 fusion
  19.1 0.3 fusion.1.own_hbm_ref.tok_ref
  19.4 0.0 copy-start.2
  19.4 0.4 collective-permute-start
  19.8 3.2 %collective-permute-done.peer_hbm_ref = bf16[1024,768]{1,0:T(8,128)(2,1)} collective-permute-done((bf16[1024,768]{1,0:T(8,128)(2,1)S(1)}, bf16[1024,768]{1,0:T(8,128)(2,1)}, u32[]{:S(2)}, u32[]{:S(2)}) %collective-permute-start) | collective-permute-done | bytes 1572896 | tf_op jit(solution)/shard_map/ppermute | solution.py:436
  23.0 33.3 %all-to-all-done.block_hbm_ref = bf16[32,24,1664]{2,1,0:T(8,128)(2,1)} async-done(((bf16[32,24,1664]{2,1,0:T(8,128)(2,1)}), bf16[32,24,1664]{2,1,0:T(8,128)(2,1)}, u32[]{:S(2)}, u32[]{:S(2)}) %all-to-all-start) | async-done | bytes 2555936 | tf_op jit(solution)/shard_map/all_to_all | solution.py:433
  56.3 0.0 copy-done.2
  56.3 17.3 %read.1 = (bf16[512,512]{1,0:T(8,128)(2,1)}, bf16[512,768]{1,0:T(8,128)(2,1)}) custom-call(s32[1]{0:T(128)} %bitcast.1.core_ref, f32[3,12]{1,0:T(4,128)} %scale_ref.3, bf16[1024,768]{1,0:T(8,128)(2,1)} %copy-done.2, bf16[1024,768]{1,0:T(8,128)(2,1)} %collective-permute-done.peer_hbm_ref, bf16[768,1664]{1,0:T(8,128)(2,1)} %bitcast.3.first_hbm_ref, ...), custom_call_target="tpu_custom_call" | custom-call | flops 20000000000 | bytes 8000000 | tf_op jit(solution)/shard_map/read/pallas_call | solution.py:351
  73.6 18.0 %all_to_all.15 = bf16[16,32,512]{2,1,0:T(8,128)(2,1)S(1)} all-to-all(bf16[16,32,512]{2,1,0:T(8,128)(2,1)} %bitcast.10), channel_id=1, replica_groups={{0,16,32,48,64,80,96,112,128,144,160,176,192,208,224,240},{8,24,40,56,7..., dimensions={0} | all-to-all | bytes 1048576 | tf_op jit(solution)/shard_map/all_to_all | solution.py:455
  91.7 1.4 combine.1
  93.1 8.1 %all-to-all-start.2 = ((bf16[32,32,384]{2,1,0:T(8,128)(2,1)}), bf16[32,32,384]{2,1,0:T(8,128)(2,1)S(1)}, u32[]{:S(2)}, u32[]{:S(2)}) async-start(bf16[32,32,384]{2,1,0:T(8,128)(2,1)} %combine.1), calls=%async_computation.2 | async-start | bytes 1572864 | tf_op jit(solution)/shard_map/all_to_all | solution.py:471
  101.2 0.0 all-gather.2.cloned.1.call-done.weight_ref.weights_ref
  101.3 0.0 copy-start.3
  101.3 1.4 copy-done.3
  102.7 0.0 copy-start.4
  102.7 0.0 copy-start.5
  102.7 3.6 %query.1.query_hbm_ref = bf16[1024,768]{1,0:T(8,128)(2,1)S(1)} custom-call(bf16[1024,768]{1,0:T(8,128)(2,1)S(1)} %copy-done.3, bf16[9,768,768]{2,1,0:T(8,128)(2,1)} %all-gather.2.cloned.1.call-done.weight_ref.weights_ref), custom_call_target="tpu_custom_call" | custom-call | flops 4000000000 | bytes 5000000 | tf_op jit(solution)/shard_map/query/pallas_call | solution.py:440
  106.3 0.0 copy-start.1
  106.3 1.1 copy-done.1
  107.4 8.1 %all-to-all-done.2 = bf16[32,32,384]{2,1,0:T(8,128)(2,1)S(1)} async-done(((bf16[32,32,384]{2,1,0:T(8,128)(2,1)}), bf16[32,32,384]{2,1,0:T(8,128)(2,1)S(1)}, u32[]{:S(2)}, u32[]{:S(2)}) %all-to-all-start.2) | async-done | bytes 786464 | tf_op jit(solution)/shard_map/all_to_all | solution.py:471
  115.5 0.0 copy-done.4
  115.5 0.0 copy-done.5
  115.5 26.1 %write.1 = (bf16[1024,768]{1,0:T(8,128)(2,1)}, f32[16,768]{1,0:T(8,128)}) custom-call(s32[1]{0:T(128)} %bitcast.index_ref, f32[3,12]{1,0:T(4,128)S(1)} %copy-done.5, bf16[16,2,32,384]{3,2,1,0:T(8,128)(2,1)S(1)} %bitcast.7, bf16[512,768]{1,0:T(8,128)(2,1)S(1)} %copy-done.4, bf16[9,768,768]{2,1,0:T(8,128)(2,1)} %all-gather.2.cloned.1.call-done.weight_ref.weights_ref, ...), custom_call_target="tpu_custom_call" | custom-call | tf_op jit(solution)/shard_map/write/pallas_call | solution.py:382
  (1 shorter events, 0.0 us)
Async XLA Ops:
  7.2 94.1 %all-gather.2.cloned.1.call-start = ((), (), s32[]{:S(2)}) async-start(), calls=%async_computation.3 | async-start | bytes 10948608 | tf_op jit(solution)/shard_map/all_gather | solution.py:434
  9.9 8.8 %copy-start = (bf16[1024,768]{1,0:T(8,128)(2,1)S(1)}, bf16[1024,768]{1,0:T(8,128)(2,1)}, u32[]{:S(2)}) copy-start(bf16[1024,768]{1,0:T(8,128)(2,1)} %raw_hbm_ref.1) | copy-start | bytes 4718596
  9.9 46.4 %all-to-all-start = ((bf16[32,24,1664]{2,1,0:T(8,128)(2,1)}), bf16[32,24,1664]{2,1,0:T(8,128)(2,1)}, u32[]{:S(2)}, u32[]{:S(2)}) async-start(bf16[32,24,1664]{2,1,0:T(8,128)(2,1)} %bitcast.9), calls=%async_computation | async-start | bytes 5111808 | tf_op jit(solution)/shard_map/all_to_all | solution.py:433
  19.4 36.9 %copy-start.2 = (bf16[1024,768]{1,0:T(8,128)(2,1)}, bf16[1024,768]{1,0:T(8,128)(2,1)S(1)}, u32[]{:S(2)}) copy-start(bf16[1024,768]{1,0:T(8,128)(2,1)S(1)} %fusion.1.own_hbm_ref.tok_ref) | copy-start | bytes 4718596
  19.4 3.6 %collective-permute-start = (bf16[1024,768]{1,0:T(8,128)(2,1)S(1)}, bf16[1024,768]{1,0:T(8,128)(2,1)}, u32[]{:S(2)}, u32[]{:S(2)}) collective-permute-start(bf16[1024,768]{1,0:T(8,128)(2,1)S(1)} %fusion.1.own_hbm_ref.tok_ref), channel_id=1, source_target_pairs={{0,8},{8,0},{16,24},{24,16},{32,40},{40,32},{48,56},{56,48},{64,72... | collective-permute-start | bytes 4718600 | tf_op jit(solution)/shard_map/ppermute | solution.py:436
  93.1 22.4 %all-to-all-start.2 = ((bf16[32,32,384]{2,1,0:T(8,128)(2,1)}), bf16[32,32,384]{2,1,0:T(8,128)(2,1)S(1)}, u32[]{:S(2)}, u32[]{:S(2)}) async-start(bf16[32,32,384]{2,1,0:T(8,128)(2,1)} %combine.1), calls=%async_computation.2 | async-start | bytes 1572864 | tf_op jit(solution)/shard_map/all_to_all | solution.py:471
  101.3 1.4 copy-start.3
  102.7 12.8 %copy-start.4 = (bf16[512,768]{1,0:T(8,128)(2,1)S(1)}, bf16[512,768]{1,0:T(8,128)(2,1)}, u32[]{:S(2)}) copy-start(bf16[512,768]{1,0:T(8,128)(2,1)} %get-tuple-element.8.lat_ref) | copy-start | bytes 2359300
  102.7 12.8 %copy-start.5 = (f32[3,12]{1,0:T(4,128)S(1)}, f32[3,12]{1,0:T(4,128)}, u32[]{:S(2)}) copy-start(f32[3,12]{1,0:T(4,128)} %scale_ref.3) | copy-start | bytes 436
  106.3 1.1 copy-start.1
Sparse Core Ops, SparseCore 0:
  10.7 88.9 all-gather.1
where the time goes:
time: 149 us; the launch traced here: 148 us
  Pallas kernels  51.1 us (34%)
  waiting for transfers between devices  44.6 us (30%)
  blocking collectives  18 us (12%)
  starting transfers between devices  17.3 us (12%)
  between operations  14.1 us (9%)
  local copies, waits for them, and re-layouts  2.55 us (2%)
    all_to_all x1, waiting for transfers between devices, shards(): first = lax.all_to_all(first, 'seq', 0, 0, tiled=True)  33.3 us
    pallas_call x1, Pallas kernels, write_call(): pl.pallas_call(write_kernel, name='write', out_shape=(jax.ShapeDtypeStruc...  26.1 us
    all_to_all x1, blocking collectives, shards(): lax.all_to_all(parts.reshape(chips, CORES * own_rows, half + PAIR), 'seq'...  18 us
    pallas_call x1, Pallas kernels, read_call(): pl.pallas_call(read_kernel, name='read', out_shape=(jax.ShapeDtypeStruct(...  17.3 us
    all_to_all x1, starting transfers between devices, shards(): first = lax.all_to_all(first, 'seq', 0, 0, tiled=True)  8.78 us
    all_to_all x1, starting transfers between devices, shards(): mixed = lax.all_to_all(mixed, 'seq', 0, 0, tiled=True)  8.13 us
    all_to_all x1, waiting for transfers between devices, shards(): mixed = lax.all_to_all(mixed, 'seq', 0, 0, tiled=True)  8.06 us
    pallas_call x1, Pallas kernels, shards(): pl.pallas_call(query_kernel, name='query', grid=(1,), out_shape=jax.Shape...  3.57 us
  transfers between devices with their start and end apart: 4, of which 3 were waited for; matrix products, arithmetic and copies ran while one was open for 0% of the time, Pallas kernels for 15%

commit v1 on v0

--- a/solution.py
+++ b/solution.py
@@ -24,7 +24,7 @@
 PIECE = 16
 TOTALS = 6
 CORES = 2
-WRITE_UNROLL = 4
+WRITE_UNROLL = 6
 
 
 def norm_rows(values):
@@ -130,12 +130,18 @@
     attend(q_ref, k_ref, v_ref, factor, emit, unroll=unroll)
 
 
-def pack_kernel(read_ref, later_ref, lat_ref, first_ref, rest_ref):
+def pack_kernel(read_ref, later_ref, lat_ref, first_ref, rest_ref, block_ref, sems):
     _, n_rows, width = read_ref.shape
     own_rows = lat_ref.shape[0]
     half = width // CORES
-    rest_ref[0] = read_ref[3]
-    rest_ref[1:] = later_ref[...]
+    n_later = later_ref.shape[0]
+    chips = first_ref.shape[0]
+    copies = [
+        pltpu.make_async_copy(read_ref.at[3], rest_ref.at[0], sems.at[chips]),
+        pltpu.make_async_copy(later_ref, rest_ref.at[pl.ds(1, n_later)], sems.at[chips + 1]),
+    ]
+    for copy in copies:
+        copy.start()
     lat = lat_ref[...].astype(F32)
     split = own_rows * width // n_rows
     low = own_rows // 2
@@ -144,7 +150,12 @@
     for core in range(CORES):
         cols = slice(core * half, (core + 1) * half)
         block = jnp.concatenate([read_ref[i][:, cols] for i in range(3)] + [extra], axis=1)
-        first_ref[:, core] = jnp.broadcast_to(block[None], (first_ref.shape[0],) + block.shape)
+        block_ref[core] = block
+    for chip in range(chips):
+        copies.append(pltpu.make_async_copy(block_ref, first_ref.at[chip], sems.at[chip]))
+        copies[-1].start()
+    for copy in copies:
+        copy.wait()
 
 
 def unpack_latents(blocks, own_rows, width):
@@ -164,6 +175,7 @@
     first_hbm_ref,
     block_hbm_ref,
     out_ref,
+    lat_hbm_ref,
     lat_ref,
     tok_ref,
     weight_ref,
@@ -199,6 +211,8 @@
     block_copy.wait()
     lat = unpack_latents(block_ref[...], n_lat // block_ref.shape[0], full_width)
     lat_ref[...] = lat.astype(BF16)
+    lat_copy = pltpu.make_async_copy(lat_ref, lat_hbm_ref, sems.at[6])
+    lat_copy.start()
     normed_ref[...] = norm_rows(lat).astype(BF16)
     weight_copies[0].wait()
     project_heads(normed_ref, weight_ref.at[:, columns[0]], mean_matrix, q_ref)
@@ -237,6 +251,7 @@
     low = extra - high - mid
     packed = high + pltpu.roll(mid, PIECE, 1) + pltpu.roll(low, 2 * PIECE, 1)
     out_ref[:, width:] = packed.astype(BF16)
+    lat_copy.wait()
 
 
 def combine_kernel(part_ref, out_ref, *, parts):
@@ -286,6 +301,7 @@
     v_ref,
     att_ref,
     write_att_ref,
+    out_ref,
     sems,
 ):
     order = (READ_OUT, SELF_Q, SELF_K, SELF_V, SELF_OUT, WRITE_K, WRITE_V, WRITE_OUT)
@@ -331,12 +347,19 @@
     attend_into(write_q_ref, k_ref, v_ref, scale_ref, 2, write_att_ref, WRITE_UNROLL)
     weight = ready(WRITE_OUT)
     raw_copy.wait()
+    out_copies = []
 
     def last(rows):
         update = dot(write_att_ref[rows, :], weight[...])
-        tok_out_ref[rows, :] = (raw_ref[rows, :].astype(F32) + update).astype(BF16)
+        out_ref[rows, :] = (raw_ref[rows, :].astype(F32) + update).astype(BF16)
+        slot = sems.at[len(order) + 2 + len(out_copies)]
+        copy = pltpu.make_async_copy(out_ref.at[rows, :], tok_out_ref.at[rows, :], slot)
+        copy.start()
+        out_copies.append(copy)
 
     row_blocks(raw_ref.shape[0], 512, last)
+    for copy in out_copies:
+        copy.wait()
 
 
 IN_VMEM = pl.BlockSpec(memory_space=pltpu.VMEM)
@@ -356,8 +379,9 @@
             jax.ShapeDtypeStruct((n_lat, width), BF16),
         ),
         in_specs=[IN_SMEM, IN_SMEM] + [IN_PLACE] * 4,
-        out_specs=(IN_VMEM, IN_VMEM),
+        out_specs=(IN_VMEM, IN_PLACE),
         scratch_shapes=[
+            pltpu.VMEM((n_lat, width), BF16),
             pltpu.VMEM((2 * n_tok, width), BF16),
             pltpu.VMEM((width, 3 * half), BF16),
             pltpu.VMEM((devices, n_rows, packed_width - 3 * half), BF16),
@@ -366,7 +390,7 @@
             pltpu.VMEM((2 * n_tok, half), BF16),
             pltpu.VMEM((2 * n_tok, half), BF16),
             pltpu.VMEM((n_lat, PAIR), F32),
-            pltpu.SemaphoreType.DMA((6,)),
+            pltpu.SemaphoreType.DMA((7,)),
         ],
         compiler_params=pltpu.CompilerParams(vmem_limit_bytes=READ_VMEM),
         cost_estimate=pl.CostEstimate(
@@ -387,7 +411,7 @@
             jax.ShapeDtypeStruct((own_rows, width), F32),
         ),
         in_specs=[IN_SMEM, IN_SMEM, IN_VMEM, IN_VMEM, IN_PLACE, IN_PLACE, IN_PLACE],
-        out_specs=(IN_VMEM, IN_VMEM),
+        out_specs=(IN_PLACE, IN_VMEM),
         scratch_shapes=[
             pltpu.VMEM((8, width, width), BF16),
             tokens_bf16,
@@ -399,7 +423,8 @@
             latents_bf16,
             latents_bf16,
             tokens_bf16,
-            pltpu.SemaphoreType.DMA((10,)),
+            tokens_bf16,
+            pltpu.SemaphoreType.DMA((12,)),
         ],
         compiler_params=pltpu.CompilerParams(vmem_limit_bytes=WRITE_VMEM),
     )(index, head_scale, mixed, lat_full, rest, tokens, queries)
@@ -425,8 +450,12 @@
             jax.ShapeDtypeStruct((chips, CORES, weight_rows, packed_width), BF16),
             jax.ShapeDtypeStruct((9, weight_rows, width), BF16),
         ),
-        in_specs=[IN_VMEM] * 3,
-        out_specs=(IN_VMEM, IN_VMEM),
+        in_specs=[IN_VMEM, IN_PLACE, IN_VMEM],
+        out_specs=(IN_PLACE, IN_PLACE),
+        scratch_shapes=[
+            pltpu.VMEM((CORES, weight_rows, packed_width), BF16),
+            pltpu.SemaphoreType.DMA((chips + 2,)),
+        ],
         compiler_params=pltpu.CompilerParams(vmem_limit_bytes=PACK_VMEM),
     )(read_weights, later_weights, latents)
     first = first.reshape(devices, weight_rows, packed_width)

time: 149 us -> 158 us (1.060)
  Pallas kernels: 51.1 us -> 59.8 us
    pallas_call x1, Pallas kernels: 2.64 us -> 11.1 us  [shards(): pl.pallas_call(pack_kernel, name='pack', out_shape=(jax.ShapeDtypeStruct(...]
  transfers between devices with their start and end apart: 4 -> 4, of which waited for: 3 -> 3; matrix products, arithmetic and copies ran while one was open for 0% -> 0% of each run, Pallas kernels for 15% -> 14%
where the time goes in v1:
time: 158 us; the launch traced here: 157 us
  Pallas kernels  59.8 us (38%)
  waiting for transfers between devices  44.9 us (28%)
  blocking collectives  18.1 us (11%)
  starting transfers between devices  17.1 us (11%)
  between operations  14.2 us (9%)
  local copies, waits for them, and re-layouts  2.55 us (2%)
    all_to_all x1, waiting for transfers between devices, shards(): first = lax.all_to_all(first, 'seq', 0, 0, tiled=True)  33.6 us
    pallas_call x1, Pallas kernels, write_call(): pl.pallas_call(write_kernel, name='write', out_shape=(jax.ShapeDtypeStruc...  26.1 us
    all_to_all x1, blocking collectives, shards(): lax.all_to_all(parts.reshape(chips, CORES * own_rows, half + PAIR), 'seq'...  18.1 us
    pallas_call x1, Pallas kernels, read_call(): pl.pallas_call(read_kernel, name='read', out_shape=(jax.ShapeDtypeStruct(...  17.6 us
    pallas_call x1, Pallas kernels, shards(): pl.pallas_call(pack_kernel, name='pack', out_shape=(jax.ShapeDtypeStruct(...  11.1 us
    all_to_all x1, starting transfers between devices, shards(): first = lax.all_to_all(first, 'seq', 0, 0, tiled=True)  8.78 us
    all_to_all x1, waiting for transfers between devices, shards(): mixed = lax.all_to_all(mixed, 'seq', 0, 0, tiled=True)  8.06 us
    all_to_all x1, starting transfers between devices, shards(): mixed = lax.all_to_all(mixed, 'seq', 0, 0, tiled=True)  7.89 us
  transfers between devices with their start and end apart: 4, of which 3 were waited for; matrix products, arithmetic and copies ran while one was open for 0% of the time, Pallas kernels for 14%

profile of v1, /device:TPU:1, one launch (start us, length us, event | category | flops | bytes accessed | tf_op | source)
XLA Modules:
  0.0 157.3 jit_solution(16167630080057264601)
XLA Ops:
  7.2 0.0 all-gather.2.cloned.1.call-start
  7.2 11.1 %pack.1 = (bf16[16,2,24,1664]{3,2,1,0:T(8,128)(2,1)}, bf16[9,24,768]{2,1,0:T(8,128)(2,1)}) custom-call(bf16[4,24,768]{2,1,0:T(8,128)(2,1)} %read_ref.1, bf16[8,24,768]{2,1,0:T(8,128)(2,1)} %later_ref.1, bf16[16,768]{1,0:T(8,128)(2,1)} %lat_ref.1), custom_call_target="tpu_custom_call" | custom-call | tf_op jit(solution)/shard_map/pack/pallas_call | solution.py:446
  18.4 0.0 all-gather.2.cloned.1.call-update
  18.4 0.0 copy-start
  18.4 8.8 %all-to-all-start = ((bf16[32,24,1664]{2,1,0:T(8,128)(2,1)}), bf16[32,24,1664]{2,1,0:T(8,128)(2,1)}, u32[]{:S(2)}, u32[]{:S(2)}) async-start(bf16[32,24,1664]{2,1,0:T(8,128)(2,1)} %bitcast.9), calls=%async_computation | async-start | bytes 5111808 | tf_op jit(solution)/shard_map/all_to_all | solution.py:462
  27.2 0.0 copy-done
  27.2 0.4 fusion
  27.6 0.3 fusion.1.own_hbm_ref.tok_ref
  27.9 0.0 copy-start.2
  27.9 0.4 collective-permute-start
  28.3 3.2 %collective-permute-done.peer_hbm_ref = bf16[1024,768]{1,0:T(8,128)(2,1)} collective-permute-done((bf16[1024,768]{1,0:T(8,128)(2,1)S(1)}, bf16[1024,768]{1,0:T(8,128)(2,1)}, u32[]{:S(2)}, u32[]{:S(2)}) %collective-permute-start) | collective-permute-done | bytes 1572896 | tf_op jit(solution)/shard_map/ppermute | solution.py:465
  31.5 33.6 %all-to-all-done.block_hbm_ref = bf16[32,24,1664]{2,1,0:T(8,128)(2,1)} async-done(((bf16[32,24,1664]{2,1,0:T(8,128)(2,1)}), bf16[32,24,1664]{2,1,0:T(8,128)(2,1)}, u32[]{:S(2)}, u32[]{:S(2)}) %all-to-all-start) | async-done | bytes 2555936 | tf_op jit(solution)/shard_map/all_to_all | solution.py:462
  65.1 0.0 copy-done.2
  65.1 17.6 %read.1 = (bf16[512,512]{1,0:T(8,128)(2,1)}, bf16[512,768]{1,0:T(8,128)(2,1)}) custom-call(s32[1]{0:T(128)} %bitcast.1.core_ref, f32[3,12]{1,0:T(4,128)} %scale_ref.3, bf16[1024,768]{1,0:T(8,128)(2,1)} %copy-done.2, bf16[1024,768]{1,0:T(8,128)(2,1)} %collective-permute-done.peer_hbm_ref, bf16[768,1664]{1,0:T(8,128)(2,1)} %bitcast.3.first_hbm_ref, ...), custom_call_target="tpu_custom_call" | custom-call | flops 20000000000 | bytes 8000000 | tf_op jit(solution)/shard_map/read/pallas_call | solution.py:374
  82.7 18.1 %all_to_all.15 = bf16[16,32,512]{2,1,0:T(8,128)(2,1)S(1)} all-to-all(bf16[16,32,512]{2,1,0:T(8,128)(2,1)} %bitcast.10), channel_id=1, replica_groups={{0,16,32,48,64,80,96,112,128,144,160,176,192,208,224,240},{8,24,40,56,7..., dimensions={0} | all-to-all | bytes 1048576 | tf_op jit(solution)/shard_map/all_to_all | solution.py:484
  100.8 1.4 combine.1
  102.2 7.9 %all-to-all-start.2 = ((bf16[32,32,384]{2,1,0:T(8,128)(2,1)}), bf16[32,32,384]{2,1,0:T(8,128)(2,1)S(1)}, u32[]{:S(2)}, u32[]{:S(2)}) async-start(bf16[32,32,384]{2,1,0:T(8,128)(2,1)} %combine.1), calls=%async_computation.2 | async-start | bytes 1572864 | tf_op jit(solution)/shard_map/all_to_all | solution.py:500
  110.1 0.0 all-gather.2.cloned.1.call-done.weight_ref.weights_ref
  110.1 0.0 copy-start.3
  110.2 1.4 copy-done.3
  111.6 0.0 copy-start.4
  111.6 0.0 copy-start.5
  111.6 3.6 %query.1.query_hbm_ref = bf16[1024,768]{1,0:T(8,128)(2,1)S(1)} custom-call(bf16[1024,768]{1,0:T(8,128)(2,1)S(1)} %copy-done.3, bf16[9,768,768]{2,1,0:T(8,128)(2,1)} %all-gather.2.cloned.1.call-done.weight_ref.weights_ref), custom_call_target="tpu_custom_call" | custom-call | flops 4000000000 | bytes 5000000 | tf_op jit(solution)/shard_map/query/pallas_call | solution.py:469
  115.1 0.0 copy-start.1
  115.2 1.1 copy-done.1
  116.3 8.1 %all-to-all-done.2 = bf16[32,32,384]{2,1,0:T(8,128)(2,1)S(1)} async-done(((bf16[32,32,384]{2,1,0:T(8,128)(2,1)}), bf16[32,32,384]{2,1,0:T(8,128)(2,1)S(1)}, u32[]{:S(2)}, u32[]{:S(2)}) %all-to-all-start.2) | async-done | bytes 786464 | tf_op jit(solution)/shard_map/all_to_all | solution.py:500
  124.3 0.0 copy-done.4
  124.3 0.0 copy-done.5
  124.3 26.1 %write.1 = (bf16[1024,768]{1,0:T(8,128)(2,1)}, f32[16,768]{1,0:T(8,128)}) custom-call(s32[1]{0:T(128)} %bitcast.index_ref, f32[3,12]{1,0:T(4,128)S(1)} %copy-done.5, bf16[16,2,32,384]{3,2,1,0:T(8,128)(2,1)S(1)} %bitcast.7, bf16[512,768]{1,0:T(8,128)(2,1)S(1)} %copy-done.4, bf16[9,768,768]{2,1,0:T(8,128)(2,1)} %all-gather.2.cloned.1.call-done.weight_ref.weights_ref, ...), custom_call_target="tpu_custom_call" | custom-call | tf_op jit(solution)/shard_map/write/pallas_call | solution.py:406
  (1 shorter events, 0.0 us)
Async XLA Ops:
  7.2 103.0 %all-gather.2.cloned.1.call-start = ((), (), s32[]{:S(2)}) async-start(), calls=%async_computation.3 | async-start | bytes 10948608 | tf_op jit(solution)/shard_map/all_gather | solution.py:463
  18.4 8.8 %copy-start = (bf16[1024,768]{1,0:T(8,128)(2,1)S(1)}, bf16[1024,768]{1,0:T(8,128)(2,1)}, u32[]{:S(2)}) copy-start(bf16[1024,768]{1,0:T(8,128)(2,1)} %raw_hbm_ref.1) | copy-start | bytes 4718596
  18.4 46.7 %all-to-all-start = ((bf16[32,24,1664]{2,1,0:T(8,128)(2,1)}), bf16[32,24,1664]{2,1,0:T(8,128)(2,1)}, u32[]{:S(2)}, u32[]{:S(2)}) async-start(bf16[32,24,1664]{2,1,0:T(8,128)(2,1)} %bitcast.9), calls=%async_computation | async-start | bytes 5111808 | tf_op jit(solution)/shard_map/all_to_all | solution.py:462
  27.9 37.2 %copy-start.2 = (bf16[1024,768]{1,0:T(8,128)(2,1)}, bf16[1024,768]{1,0:T(8,128)(2,1)S(1)}, u32[]{:S(2)}) copy-start(bf16[1024,768]{1,0:T(8,128)(2,1)S(1)} %fusion.1.own_hbm_ref.tok_ref) | copy-start | bytes 4718596
  27.9 3.6 %collective-permute-start = (bf16[1024,768]{1,0:T(8,128)(2,1)S(1)}, bf16[1024,768]{1,0:T(8,128)(2,1)}, u32[]{:S(2)}, u32[]{:S(2)}) collective-permute-start(bf16[1024,768]{1,0:T(8,128)(2,1)S(1)} %fusion.1.own_hbm_ref.tok_ref), channel_id=1, source_target_pairs={{0,8},{8,0},{16,24},{24,16},{32,40},{40,32},{48,56},{56,48},{64,72... | collective-permute-start | bytes 4718600 | tf_op jit(solution)/shard_map/ppermute | solution.py:465
  102.2 22.1 %all-to-all-start.2 = ((bf16[32,32,384]{2,1,0:T(8,128)(2,1)}), bf16[32,32,384]{2,1,0:T(8,128)(2,1)S(1)}, u32[]{:S(2)}, u32[]{:S(2)}) async-start(bf16[32,32,384]{2,1,0:T(8,128)(2,1)} %combine.1), calls=%async_computation.2 | async-start | bytes 1572864 | tf_op jit(solution)/shard_map/all_to_all | solution.py:500
  110.1 1.4 copy-start.3
  111.6 12.8 %copy-start.4 = (bf16[512,768]{1,0:T(8,128)(2,1)S(1)}, bf16[512,768]{1,0:T(8,128)(2,1)}, u32[]{:S(2)}) copy-start(bf16[512,768]{1,0:T(8,128)(2,1)} %get-tuple-element.8.lat_ref) | copy-start | bytes 2359300
  111.6 12.8 %copy-start.5 = (f32[3,12]{1,0:T(4,128)S(1)}, f32[3,12]{1,0:T(4,128)}, u32[]{:S(2)}) copy-start(f32[3,12]{1,0:T(4,128)} %scale_ref.3) | copy-start | bytes 436
  115.1 1.1 copy-start.1
Sparse Core Ops, SparseCore 0:
  18.5 89.5 all-gather.1

commit v2 on v0

--- a/solution.py
+++ b/solution.py
@@ -24,7 +24,7 @@
 PIECE = 16
 TOTALS = 6
 CORES = 2
-WRITE_UNROLL = 4
+WRITE_UNROLL = 12
 
 
 def norm_rows(values):

time: 149 us -> 148 us (level)
  no operation moved by 1% of the time
where the time goes in v2:
time: 148 us; the launch traced here: 147 us
  Pallas kernels  49.7 us (34%)
  waiting for transfers between devices  44.6 us (30%)
  blocking collectives  18 us (12%)
  starting transfers between devices  17.3 us (12%)
  between operations  14.1 us (10%)
  local copies, waits for them, and re-layouts  2.55 us (2%)
    all_to_all x1, waiting for transfers between devices, shards(): first = lax.all_to_all(first, 'seq', 0, 0, tiled=True)  33.3 us
    pallas_call x1, Pallas kernels, write_call(): pl.pallas_call(write_kernel, name='write', out_shape=(jax.ShapeDtypeStruc...  24.8 us
    all_to_all x1, blocking collectives, shards(): lax.all_to_all(parts.reshape(chips, CORES * own_rows, half + PAIR), 'seq'...  18 us
    pallas_call x1, Pallas kernels, read_call(): pl.pallas_call(read_kernel, name='read', out_shape=(jax.ShapeDtypeStruct(...  17.3 us
    all_to_all x1, starting transfers between devices, shards(): first = lax.all_to_all(first, 'seq', 0, 0, tiled=True)  8.78 us
    all_to_all x1, starting transfers between devices, shards(): mixed = lax.all_to_all(mixed, 'seq', 0, 0, tiled=True)  8.12 us
    all_to_all x1, waiting for transfers between devices, shards(): mixed = lax.all_to_all(mixed, 'seq', 0, 0, tiled=True)  8.07 us
    pallas_call x1, Pallas kernels, shards(): pl.pallas_call(query_kernel, name='query', grid=(1,), out_shape=jax.Shape...  3.57 us
  transfers between devices with their start and end apart: 4, of which 3 were waited for; matrix products, arithmetic and copies ran while one was open for 0% of the time, Pallas kernels for 15%

profile of v2, /device:TPU:1, one launch (start us, length us, event | category | flops | bytes accessed | tf_op | source)
XLA Modules:
  0.0 147.1 jit_solution(12052290691160916336)
XLA Ops:
  7.2 0.0 all-gather.2.cloned.1.call-start
  7.2 2.6 %pack.1 = (bf16[16,2,24,1664]{3,2,1,0:T(8,128)(2,1)}, bf16[9,24,768]{2,1,0:T(8,128)(2,1)}) custom-call(bf16[4,24,768]{2,1,0:T(8,128)(2,1)} %read_ref.1, bf16[8,24,768]{2,1,0:T(8,128)(2,1)} %later_ref.1, bf16[16,768]{1,0:T(8,128)(2,1)} %lat_ref.1), custom_call_target="tpu_custom_call" | custom-call | tf_op jit(solution)/shard_map/pack/pallas_call | solution.py:421
  9.8 0.0 all-gather.2.cloned.1.call-update
  9.9 0.0 copy-start
  9.9 8.8 %all-to-all-start = ((bf16[32,24,1664]{2,1,0:T(8,128)(2,1)}), bf16[32,24,1664]{2,1,0:T(8,128)(2,1)}, u32[]{:S(2)}, u32[]{:S(2)}) async-start(bf16[32,24,1664]{2,1,0:T(8,128)(2,1)} %bitcast.9), calls=%async_computation | async-start | bytes 5111808 | tf_op jit(solution)/shard_map/all_to_all | solution.py:433
  18.7 0.0 copy-done
  18.7 0.4 fusion
  19.1 0.3 fusion.1.own_hbm_ref.tok_ref
  19.4 0.0 copy-start.2
  19.4 0.4 collective-permute-start
  19.8 3.2 %collective-permute-done.peer_hbm_ref = bf16[1024,768]{1,0:T(8,128)(2,1)} collective-permute-done((bf16[1024,768]{1,0:T(8,128)(2,1)S(1)}, bf16[1024,768]{1,0:T(8,128)(2,1)}, u32[]{:S(2)}, u32[]{:S(2)}) %collective-permute-start) | collective-permute-done | bytes 1572896 | tf_op jit(solution)/shard_map/ppermute | solution.py:436
  23.0 33.3 %all-to-all-done.block_hbm_ref = bf16[32,24,1664]{2,1,0:T(8,128)(2,1)} async-done(((bf16[32,24,1664]{2,1,0:T(8,128)(2,1)}), bf16[32,24,1664]{2,1,0:T(8,128)(2,1)}, u32[]{:S(2)}, u32[]{:S(2)}) %all-to-all-start) | async-done | bytes 2555936 | tf_op jit(solution)/shard_map/all_to_all | solution.py:433
  56.3 0.0 copy-done.2
  56.3 17.3 %read.1 = (bf16[512,512]{1,0:T(8,128)(2,1)}, bf16[512,768]{1,0:T(8,128)(2,1)}) custom-call(s32[1]{0:T(128)} %bitcast.1.core_ref, f32[3,12]{1,0:T(4,128)} %scale_ref.3, bf16[1024,768]{1,0:T(8,128)(2,1)} %copy-done.2, bf16[1024,768]{1,0:T(8,128)(2,1)} %collective-permute-done.peer_hbm_ref, bf16[768,1664]{1,0:T(8,128)(2,1)} %bitcast.3.first_hbm_ref, ...), custom_call_target="tpu_custom_call" | custom-call | flops 20000000000 | bytes 8000000 | tf_op jit(solution)/shard_map/read/pallas_call | solution.py:351
  73.6 18.0 %all_to_all.15 = bf16[16,32,512]{2,1,0:T(8,128)(2,1)S(1)} all-to-all(bf16[16,32,512]{2,1,0:T(8,128)(2,1)} %bitcast.10), channel_id=1, replica_groups={{0,16,32,48,64,80,96,112,128,144,160,176,192,208,224,240},{8,24,40,56,7..., dimensions={0} | all-to-all | bytes 1048576 | tf_op jit(solution)/shard_map/all_to_all | solution.py:455
  91.7 1.4 combine.1
  93.1 8.1 %all-to-all-start.2 = ((bf16[32,32,384]{2,1,0:T(8,128)(2,1)}), bf16[32,32,384]{2,1,0:T(8,128)(2,1)S(1)}, u32[]{:S(2)}, u32[]{:S(2)}) async-start(bf16[32,32,384]{2,1,0:T(8,128)(2,1)} %combine.1), calls=%async_computation.2 | async-start | bytes 1572864 | tf_op jit(solution)/shard_map/all_to_all | solution.py:471
  101.2 0.0 all-gather.2.cloned.1.call-done.weight_ref.weights_ref
  101.3 0.0 copy-start.3
  101.3 1.4 copy-done.3
  102.7 0.0 copy-start.4
  102.7 0.0 copy-start.5
  102.7 3.6 %query.1.query_hbm_ref = bf16[1024,768]{1,0:T(8,128)(2,1)S(1)} custom-call(bf16[1024,768]{1,0:T(8,128)(2,1)S(1)} %copy-done.3, bf16[9,768,768]{2,1,0:T(8,128)(2,1)} %all-gather.2.cloned.1.call-done.weight_ref.weights_ref), custom_call_target="tpu_custom_call" | custom-call | flops 4000000000 | bytes 5000000 | tf_op jit(solution)/shard_map/query/pallas_call | solution.py:440
  106.3 0.0 copy-start.1
  106.3 1.1 copy-done.1
  107.4 8.1 %all-to-all-done.2 = bf16[32,32,384]{2,1,0:T(8,128)(2,1)S(1)} async-done(((bf16[32,32,384]{2,1,0:T(8,128)(2,1)}), bf16[32,32,384]{2,1,0:T(8,128)(2,1)S(1)}, u32[]{:S(2)}, u32[]{:S(2)}) %all-to-all-start.2) | async-done | bytes 786464 | tf_op jit(solution)/shard_map/all_to_all | solution.py:471
  115.5 0.0 copy-done.4
  115.5 0.0 copy-done.5
  115.5 24.8 %write.1 = (bf16[1024,768]{1,0:T(8,128)(2,1)}, f32[16,768]{1,0:T(8,128)}) custom-call(s32[1]{0:T(128)} %bitcast.index_ref, f32[3,12]{1,0:T(4,128)S(1)} %copy-done.5, bf16[16,2,32,384]{3,2,1,0:T(8,128)(2,1)S(1)} %bitcast.7, bf16[512,768]{1,0:T(8,128)(2,1)S(1)} %copy-done.4, bf16[9,768,768]{2,1,0:T(8,128)(2,1)} %all-gather.2.cloned.1.call-done.weight_ref.weights_ref, ...), custom_call_target="tpu_custom_call" | custom-call | tf_op jit(solution)/shard_map/write/pallas_call | solution.py:382
  (1 shorter events, 0.0 us)
Async XLA Ops:
  7.2 94.1 %all-gather.2.cloned.1.call-start = ((), (), s32[]{:S(2)}) async-start(), calls=%async_computation.3 | async-start | bytes 10948608 | tf_op jit(solution)/shard_map/all_gather | solution.py:434
  9.9 8.8 %copy-start = (bf16[1024,768]{1,0:T(8,128)(2,1)S(1)}, bf16[1024,768]{1,0:T(8,128)(2,1)}, u32[]{:S(2)}) copy-start(bf16[1024,768]{1,0:T(8,128)(2,1)} %raw_hbm_ref.1) | copy-start | bytes 4718596
  9.9 46.4 %all-to-all-start = ((bf16[32,24,1664]{2,1,0:T(8,128)(2,1)}), bf16[32,24,1664]{2,1,0:T(8,128)(2,1)}, u32[]{:S(2)}, u32[]{:S(2)}) async-start(bf16[32,24,1664]{2,1,0:T(8,128)(2,1)} %bitcast.9), calls=%async_computation | async-start | bytes 5111808 | tf_op jit(solution)/shard_map/all_to_all | solution.py:433
  19.4 36.9 %copy-start.2 = (bf16[1024,768]{1,0:T(8,128)(2,1)}, bf16[1024,768]{1,0:T(8,128)(2,1)S(1)}, u32[]{:S(2)}) copy-start(bf16[1024,768]{1,0:T(8,128)(2,1)S(1)} %fusion.1.own_hbm_ref.tok_ref) | copy-start | bytes 4718596
  19.4 3.6 %collective-permute-start = (bf16[1024,768]{1,0:T(8,128)(2,1)S(1)}, bf16[1024,768]{1,0:T(8,128)(2,1)}, u32[]{:S(2)}, u32[]{:S(2)}) collective-permute-start(bf16[1024,768]{1,0:T(8,128)(2,1)S(1)} %fusion.1.own_hbm_ref.tok_ref), channel_id=1, source_target_pairs={{0,8},{8,0},{16,24},{24,16},{32,40},{40,32},{48,56},{56,48},{64,72... | collective-permute-start | bytes 4718600 | tf_op jit(solution)/shard_map/ppermute | solution.py:436
  93.1 22.4 %all-to-all-start.2 = ((bf16[32,32,384]{2,1,0:T(8,128)(2,1)}), bf16[32,32,384]{2,1,0:T(8,128)(2,1)S(1)}, u32[]{:S(2)}, u32[]{:S(2)}) async-start(bf16[32,32,384]{2,1,0:T(8,128)(2,1)} %combine.1), calls=%async_computation.2 | async-start | bytes 1572864 | tf_op jit(solution)/shard_map/all_to_all | solution.py:471
  101.3 1.4 copy-start.3
  102.7 12.8 %copy-start.4 = (bf16[512,768]{1,0:T(8,128)(2,1)S(1)}, bf16[512,768]{1,0:T(8,128)(2,1)}, u32[]{:S(2)}) copy-start(bf16[512,768]{1,0:T(8,128)(2,1)} %get-tuple-element.8.lat_ref) | copy-start | bytes 2359300
  102.7 12.8 %copy-start.5 = (f32[3,12]{1,0:T(4,128)S(1)}, f32[3,12]{1,0:T(4,128)}, u32[]{:S(2)}) copy-start(f32[3,12]{1,0:T(4,128)} %scale_ref.3) | copy-start | bytes 436
  106.3 1.1 copy-start.1
Sparse Core Ops, SparseCore 0:
  10.7 88.9 all-gather.1

commit v3 on v2

--- a/solution.py
+++ b/solution.py
@@ -17,7 +17,7 @@
 F32 = jnp.float32
 MIB = 1024 * 1024
 PACK_VMEM = 58 * MIB
-READ_VMEM = 56 * MIB
+READ_VMEM = 40 * MIB
 COMBINE_VMEM = 40 * MIB
 QUERY_VMEM = 50 * MIB
 WRITE_VMEM = 50 * MIB
@@ -164,6 +164,7 @@
     first_hbm_ref,
     block_hbm_ref,
     out_ref,
+    lat_hbm_ref,
     lat_ref,
     tok_ref,
     weight_ref,
@@ -199,6 +200,8 @@
     block_copy.wait()
     lat = unpack_latents(block_ref[...], n_lat // block_ref.shape[0], full_width)
     lat_ref[...] = lat.astype(BF16)
+    lat_copy = pltpu.make_async_copy(lat_ref, lat_hbm_ref, sems.at[6])
+    lat_copy.start()
     normed_ref[...] = norm_rows(lat).astype(BF16)
     weight_copies[0].wait()
     project_heads(normed_ref, weight_ref.at[:, columns[0]], mean_matrix, q_ref)
@@ -237,6 +240,7 @@
     low = extra - high - mid
     packed = high + pltpu.roll(mid, PIECE, 1) + pltpu.roll(low, 2 * PIECE, 1)
     out_ref[:, width:] = packed.astype(BF16)
+    lat_copy.wait()
 
 
 def combine_kernel(part_ref, out_ref, *, parts):
@@ -356,8 +360,9 @@
             jax.ShapeDtypeStruct((n_lat, width), BF16),
         ),
         in_specs=[IN_SMEM, IN_SMEM] + [IN_PLACE] * 4,
-        out_specs=(IN_VMEM, IN_VMEM),
+        out_specs=(IN_VMEM, pl.BlockSpec(memory_space=pltpu.HBM)),
         scratch_shapes=[
+            pltpu.VMEM((n_lat, width), BF16),
             pltpu.VMEM((2 * n_tok, width), BF16),
             pltpu.VMEM((width, 3 * half), BF16),
             pltpu.VMEM((devices, n_rows, packed_width - 3 * half), BF16),
@@ -366,7 +371,7 @@
             pltpu.VMEM((2 * n_tok, half), BF16),
             pltpu.VMEM((2 * n_tok, half), BF16),
             pltpu.VMEM((n_lat, PAIR), F32),
-            pltpu.SemaphoreType.DMA((6,)),
+            pltpu.SemaphoreType.DMA((7,)),
         ],
         compiler_params=pltpu.CompilerParams(vmem_limit_bytes=READ_VMEM),
         cost_estimate=pl.CostEstimate(

time: 148 us -> 147 us (level)
    unnamed x12 -> x14, local copies, waits for them, and re-layouts: 2.55 us -> 3.46 us
  transfers between devices with their start and end apart: 4 -> 4, of which waited for: 3 -> 3; matrix products, arithmetic and copies ran while one was open for 0% -> 0% of each run, Pallas kernels for 15% -> 14%
where the time goes in v3:
time: 147 us
  Pallas kernels  48.8 us (33%)
  waiting for transfers between devices  44.6 us (30%)
  blocking collectives  17.9 us (12%)
  starting transfers between devices  17.3 us (12%)
  between operations  14.2 us (10%)
  local copies, waits for them, and re-layouts  3.46 us (2%)
    all_to_all x1, waiting for transfers between devices, shards(): first = lax.all_to_all(first, 'seq', 0, 0, tiled=True)  33.3 us
    pallas_call x1, Pallas kernels, write_call(): pl.pallas_call(write_kernel, name='write', out_shape=(jax.ShapeDtypeStruc...  24.8 us
    all_to_all x1, blocking collectives, shards(): lax.all_to_all(parts.reshape(chips, CORES * own_rows, half + PAIR), 'seq'...  17.9 us
    pallas_call x1, Pallas kernels, read_call(): pl.pallas_call(read_kernel, name='read', out_shape=(jax.ShapeDtypeStruct(...  16.2 us
    all_to_all x1, starting transfers between devices, shards(): first = lax.all_to_all(first, 'seq', 0, 0, tiled=True)  8.78 us
    all_to_all x1, starting transfers between devices, shards(): mixed = lax.all_to_all(mixed, 'seq', 0, 0, tiled=True)  8.12 us
    all_to_all x1, waiting for transfers between devices, shards(): mixed = lax.all_to_all(mixed, 'seq', 0, 0, tiled=True)  8.04 us
    pallas_call x1, Pallas kernels, shards(): pl.pallas_call(query_kernel, name='query', grid=(1,), out_shape=jax.Shape...  3.6 us
  transfers between devices with their start and end apart: 4, of which 3 were waited for; matrix products, arithmetic and copies ran while one was open for 0% of the time, Pallas kernels for 14%

profile of v3, /device:TPU:1, one launch (start us, length us, event | category | flops | bytes accessed | tf_op | source)
XLA Modules:
  0.0 146.9 jit_solution(15930353587096541583)
XLA Ops:
  7.2 0.0 all-gather.2.cloned.1.call-start
  7.2 2.8 %pack.1 = (bf16[16,2,24,1664]{3,2,1,0:T(8,128)(2,1)}, bf16[9,24,768]{2,1,0:T(8,128)(2,1)}) custom-call(bf16[4,24,768]{2,1,0:T(8,128)(2,1)} %read_ref.1, bf16[8,24,768]{2,1,0:T(8,128)(2,1)} %later_ref.1, bf16[16,768]{1,0:T(8,128)(2,1)} %lat_ref.1), custom_call_target="tpu_custom_call" | custom-call | tf_op jit(solution)/shard_map/pack/pallas_call | solution.py:426
  10.0 0.0 all-gather.2.cloned.1.call-update
  10.0 0.0 copy-start
  10.0 8.8 %all-to-all-start = ((bf16[32,24,1664]{2,1,0:T(8,128)(2,1)}), bf16[32,24,1664]{2,1,0:T(8,128)(2,1)}, u32[]{:S(2)}, u32[]{:S(2)}) async-start(bf16[32,24,1664]{2,1,0:T(8,128)(2,1)} %bitcast.10), calls=%async_computation | async-start | bytes 5111808 | tf_op jit(solution)/shard_map/all_to_all | solution.py:438
  18.8 0.0 copy-done
  18.8 0.0 copy-start.6
  18.8 0.4 fusion
  19.2 0.3 fusion.1.own_hbm_ref.tok_ref
  19.5 0.0 copy-start.2
  19.6 0.4 collective-permute-start
  19.9 3.2 %collective-permute-done.peer_hbm_ref = bf16[1024,768]{1,0:T(8,128)(2,1)} collective-permute-done((bf16[1024,768]{1,0:T(8,128)(2,1)S(1)}, bf16[1024,768]{1,0:T(8,128)(2,1)}, u32[]{:S(2)}, u32[]{:S(2)}) %collective-permute-start) | collective-permute-done | bytes 1572896 | tf_op jit(solution)/shard_map/ppermute | solution.py:441
  23.2 33.3 %all-to-all-done.block_hbm_ref = bf16[32,24,1664]{2,1,0:T(8,128)(2,1)} async-done(((bf16[32,24,1664]{2,1,0:T(8,128)(2,1)}), bf16[32,24,1664]{2,1,0:T(8,128)(2,1)}, u32[]{:S(2)}, u32[]{:S(2)}) %all-to-all-start) | async-done | bytes 2555936 | tf_op jit(solution)/shard_map/all_to_all | solution.py:438
  56.5 0.0 copy-done.6
  56.5 16.2 %read.1 = (bf16[512,512]{1,0:T(8,128)(2,1)S(1)}, bf16[512,768]{1,0:T(8,128)(2,1)S(1)}) custom-call(s32[1]{0:T(128)} %bitcast.1.core_ref, f32[3,12]{1,0:T(4,128)S(1)} %copy-done.6, bf16[1024,768]{1,0:T(8,128)(2,1)S(1)} %fusion.1.own_hbm_ref.tok_ref, bf16[1024,768]{1,0:T(8,128)(2,1)} %collective-permute-done.peer_hbm_ref, ...), custom_call_target="tpu_custom_call" | custom-call | flops 20000000000 | bytes 8000000 | tf_op jit(solution)/shard_map/read/pallas_call | solution.py:355
  72.7 0.0 copy-done.2
  72.7 0.0 copy-start.4
  72.7 0.9 copy-done.4
  73.6 17.9 %all_to_all.15 = bf16[16,32,512]{2,1,0:T(8,128)(2,1)S(1)} all-to-all(bf16[16,32,512]{2,1,0:T(8,128)(2,1)S(1)} %bitcast.9), channel_id=1, replica_groups={{0,16,32,48,64,80,96,112,128,144,160,176,192,208,224,240},{8,24,40,56,7..., dimensions={0} | all-to-all | bytes 1048576 | tf_op jit(solution)/shard_map/all_to_all | solution.py:460
  91.4 1.4 combine.1
  92.9 8.1 %all-to-all-start.2 = ((bf16[32,32,384]{2,1,0:T(8,128)(2,1)}), bf16[32,32,384]{2,1,0:T(8,128)(2,1)S(1)}, u32[]{:S(2)}, u32[]{:S(2)}) async-start(bf16[32,32,384]{2,1,0:T(8,128)(2,1)} %combine.1), calls=%async_computation.2 | async-start | bytes 1572864 | tf_op jit(solution)/shard_map/all_to_all | solution.py:476
  101.0 0.0 all-gather.2.cloned.1.call-done.weight_ref.weights_ref
  101.0 0.0 copy-start.3
  101.0 1.4 copy-done.3
  102.4 0.0 copy-start.5
  102.4 3.6 %query.1.query_hbm_ref = bf16[1024,768]{1,0:T(8,128)(2,1)S(1)} custom-call(bf16[1024,768]{1,0:T(8,128)(2,1)S(1)} %copy-done.3, bf16[9,768,768]{2,1,0:T(8,128)(2,1)} %all-gather.2.cloned.1.call-done.weight_ref.weights_ref), custom_call_target="tpu_custom_call" | custom-call | flops 4000000000 | bytes 5000000 | tf_op jit(solution)/shard_map/query/pallas_call | solution.py:445
  106.0 0.0 copy-start.1
  106.1 1.1 copy-done.1
  107.2 8.0 %all-to-all-done.2 = bf16[32,32,384]{2,1,0:T(8,128)(2,1)S(1)} async-done(((bf16[32,32,384]{2,1,0:T(8,128)(2,1)}), bf16[32,32,384]{2,1,0:T(8,128)(2,1)S(1)}, u32[]{:S(2)}, u32[]{:S(2)}) %all-to-all-start.2) | async-done | bytes 786464 | tf_op jit(solution)/shard_map/all_to_all | solution.py:476
  115.2 0.0 copy-done.5
  115.2 24.8 %write.1 = (bf16[1024,768]{1,0:T(8,128)(2,1)}, f32[16,768]{1,0:T(8,128)}) custom-call(s32[1]{0:T(128)} %bitcast.index_ref, f32[3,12]{1,0:T(4,128)S(1)} %copy-done.6, bf16[16,2,32,384]{3,2,1,0:T(8,128)(2,1)S(1)} %bitcast.7, bf16[512,768]{1,0:T(8,128)(2,1)S(1)} %copy-done.5, bf16[9,768,768]{2,1,0:T(8,128)(2,1)} %all-gather.2.cloned.1.call-done.weight_ref.weights_ref, ...), custom_call_target="tpu_custom_call" | custom-call | tf_op jit(solution)/shard_map/write/pallas_call | solution.py:387
  (1 shorter events, 0.0 us)
Async XLA Ops:
  7.2 93.9 %all-gather.2.cloned.1.call-start = ((), (), s32[]{:S(2)}) async-start(), calls=%async_computation.3 | async-start | bytes 10948608 | tf_op jit(solution)/shard_map/all_gather | solution.py:439
  10.0 8.8 %copy-start = (bf16[1024,768]{1,0:T(8,128)(2,1)S(1)}, bf16[1024,768]{1,0:T(8,128)(2,1)}, u32[]{:S(2)}) copy-start(bf16[1024,768]{1,0:T(8,128)(2,1)} %raw_hbm_ref.1) | copy-start | bytes 4718596
  10.0 46.5 %all-to-all-start = ((bf16[32,24,1664]{2,1,0:T(8,128)(2,1)}), bf16[32,24,1664]{2,1,0:T(8,128)(2,1)}, u32[]{:S(2)}, u32[]{:S(2)}) async-start(bf16[32,24,1664]{2,1,0:T(8,128)(2,1)} %bitcast.10), calls=%async_computation | async-start | bytes 5111808 | tf_op jit(solution)/shard_map/all_to_all | solution.py:438
  18.8 37.7 %copy-start.6 = (f32[3,12]{1,0:T(4,128)S(1)}, f32[3,12]{1,0:T(4,128)}, u32[]{:S(2)}) copy-start(f32[3,12]{1,0:T(4,128)} %scale_ref.3) | copy-start | bytes 436
  19.5 53.1 %copy-start.2 = (bf16[1024,768]{1,0:T(8,128)(2,1)}, bf16[1024,768]{1,0:T(8,128)(2,1)S(1)}, u32[]{:S(2)}) copy-start(bf16[1024,768]{1,0:T(8,128)(2,1)S(1)} %fusion.1.own_hbm_ref.tok_ref) | copy-start | bytes 4718596
  19.6 3.6 %collective-permute-start = (bf16[1024,768]{1,0:T(8,128)(2,1)S(1)}, bf16[1024,768]{1,0:T(8,128)(2,1)}, u32[]{:S(2)}, u32[]{:S(2)}) collective-permute-start(bf16[1024,768]{1,0:T(8,128)(2,1)S(1)} %fusion.1.own_hbm_ref.tok_ref), channel_id=1, source_target_pairs={{0,8},{8,0},{16,24},{24,16},{32,40},{40,32},{48,56},{56,48},{64,72... | collective-permute-start | bytes 4718600 | tf_op jit(solution)/shard_map/ppermute | solution.py:441
  72.7 0.9 copy-start.4
  92.9 22.3 %all-to-all-start.2 = ((bf16[32,32,384]{2,1,0:T(8,128)(2,1)}), bf16[32,32,384]{2,1,0:T(8,128)(2,1)S(1)}, u32[]{:S(2)}, u32[]{:S(2)}) async-start(bf16[32,32,384]{2,1,0:T(8,128)(2,1)} %combine.1), calls=%async_computation.2 | async-start | bytes 1572864 | tf_op jit(solution)/shard_map/all_to_all | solution.py:476
  101.0 1.4 copy-start.3
  102.4 12.8 %copy-start.5 = (bf16[512,768]{1,0:T(8,128)(2,1)S(1)}, bf16[512,768]{1,0:T(8,128)(2,1)}, u32[]{:S(2)}) copy-start(bf16[512,768]{1,0:T(8,128)(2,1)} %copy-done.4) | copy-start | bytes 2359300
  106.0 1.1 copy-start.1
Sparse Core Ops, SparseCore 0:
  10.7 89.0 all-gather.1
